TPU v7x, 1024 devices: a whole 4x4x32 slice. The times are simulated.
1024 devices in a mesh: rep: 128 (over y_hi, z, core), fsdp: 8 (over x, y_lo).
Axes of the slice: x: 4, y: 4 (y_hi: 2, y_lo: 2; y = y_hi * 2 + y_lo), z: 32, core: 2. Of those that a mesh axis runs over, the one named last changes fastest.
Arguments:
- activations: bfloat16 [65536, 8192], P('rep'), may hold values from -6 to 6
- key_cotangent: bfloat16 [65536, 1024], P('rep', 'fsdp'), may hold values from -0.25 to 0.25
- deltas: bfloat16 [128, 512, 1024], P('rep', None, 'fsdp'), may hold values from -24 to 24
- delta_scales: int32 [128, 512, 8], P('rep', None, 'fsdp'), may hold values from -3 to 0
- global_copy: float32 [512, 1024], P(None, 'fsdp'), may hold values from -0.75 to 0.75
- momentum: float32 [512, 1024], P(None, 'fsdp'), may hold values from -0.75 to 0.75
- code_scales: int32 [512, 8], P(None, 'fsdp'), may hold values from -6 to -3
Outputs:
- key_grad: bfloat16 [128, 8192, 1024], P('rep', None, 'fsdp')
- new_momentum: float32 [512, 1024], P('rep', 'fsdp')
- new_global: float32 [512, 1024], P('rep', 'fsdp')
- encoded: bfloat16 [512, 1024], P(None, 'fsdp')
All inputs are finite; a program needn't handle non-finite values.
Results may differ from a plain program's by a relative error of at most 0.001.
Values may be sent and summed in bfloat16 or wider, within the bound.
No kernel may reach another device: no remote copies, remote signals or barrier semaphores. Data moves between devices by JAX's collectives and lax.ppermute only.
A program may use at most 32 MiB of HBM per device.

v0:
```python
import jax
import jax.numpy as jnp
from jax import lax
from jax.sharding import PartitionSpec as P

outer_rate = 0.7
decay_rate = 0.9


def decode_block(coded, scales):
    row_count = coded.shape[0]
    blocked = coded.astype(jnp.float32).reshape(row_count, -1, 128)
    blocked = blocked * jnp.exp2(scales.astype(jnp.float32))[:, :, None]
    return blocked.reshape(row_count, -1)


def shards(activations, key_cotangent, deltas, delta_scales, global_copy, momentum, code_scales):
    key_grad = lax.dot_general(
        activations, key_cotangent, (((0,), (0,)), ((), ())), preferred_element_type=jnp.float32
    )
    key_grad = key_grad.astype(jnp.bfloat16)[None]
    local_codes = deltas[0]
    local_scales = delta_scales[0]
    all_rows = local_codes.shape[0]
    share_rows = all_rows // lax.axis_size("rep")
    row_first = lax.axis_index("rep") * share_rows
    summed = lax.psum_scatter(
        decode_block(local_codes, local_scales), "rep", scatter_dimension=0, tiled=True
    )
    moment_rows = lax.dynamic_slice_in_dim(momentum, row_first, share_rows, 0)
    global_rows = lax.dynamic_slice_in_dim(global_copy, row_first, share_rows, 0)
    scale_rows = lax.dynamic_slice_in_dim(code_scales, row_first, share_rows, 0)
    outer_grad = -summed / lax.axis_size("rep")
    new_momentum = decay_rate * moment_rows + outer_grad
    new_global = global_rows - outer_rate * (outer_grad + decay_rate * new_momentum)
    coded_share = decode_block(new_global, -scale_rows).astype(jnp.bfloat16)
    encoded = lax.all_gather(coded_share, "rep", axis=0, tiled=True)
    return (key_grad, new_momentum, new_global, encoded)


def solution(mesh):
    in_specs = (
        P("rep", None),
        P("rep", "fsdp"),
        P("rep", None, "fsdp"),
        P("rep", None, "fsdp"),
        P(None, "fsdp"),
        P(None, "fsdp"),
        P(None, "fsdp"),
    )
    out_specs = (P("rep", None, "fsdp"), P("rep", "fsdp"), P("rep", "fsdp"), P(None, "fsdp"))
    return jax.shard_map(shards, mesh=mesh, in_specs=in_specs, out_specs=out_specs, check_vma=False)
```

profile of v0, /device:TPU:1, one launch (start us, length us, event | category | flops | bytes accessed | tf_op | source)
XLA Modules:
  0.0 1072.7 jit_solution(15658796350054013309)
XLA Ops:
  7.2 0.0 copy-start
  7.2 0.0 all-reduce.3.cloned.1.call-start
  7.2 0.7 multiply_exponential_fusion
  7.9 1.7 convert_multiply_fusion
  9.7 0.0 all-reduce.3.cloned.1.call-update
  9.7 0.0 copy-done
  9.7 7.1 fusion
  16.8 1.3 dynamic-slice
  18.8 0.7 exponential_bitcast_fusion
  19.5 902.3 %all-reduce.3.cloned.1.call-done = f32[512,128]{1,0:T(8,128)} async-done(((f32[512,128]{1,0:T(8,128)}), f32[512,128]{1,0:T(8,128)}) %all-reduce.3.cloned.1.call-update) | async-done | bytes 262160
  921.8 1.3 fusion.2
  923.1 142.1 %all-gather = bf16[128,4,128]{2,1,0:T(4,128)(2,1)S(1)} all-gather(bf16[1,4,128]{2,1,0:T(4,128)(2,1)S(1)} %get-tuple-element.4), channel_id=1, replica_groups=mesh['rep'=128,'fsdp'=8] {'rep'}, dimensions={0}, use_global_device_ids=true | all-gather | bytes 132096 | tf_op jit(solution)/shard_map/all_gather | solution.py:37
  1065.2 0.7 copy.13
Async XLA Ops:
  7.2 2.6 copy-start
  7.2 914.7 %all-reduce.3.cloned.1.call-start = ((), (), s32[]{:S(2)}) async-start(), calls=%async_computation | async-start | bytes 524288
Sparse Core Ops, SparseCore 0:
  11.5 910.2 all-reduce.2
where the time goes:
time: 1070 us
  waiting for transfers between devices  902 us (84%)
  blocking collectives  142 us (13%)
  between operations  14.7 us (1%)
    unnamed x2, waiting for transfers between devices  902 us
    all_gather x1, blocking collectives, shards(): encoded = lax.all_gather(coded_share, 'rep', axis=0, tiled=True)  142 us
  transfers between devices with their start and end apart: 1, of which 1 were waited for; matrix products, arithmetic and copies ran while one was open for 1% of the time, Pallas kernels for 0%

commit v1 on v0

v1 whole, which is shorter than its diff:
```python
import jax
import jax.numpy as jnp
import numpy as np
from jax import lax
from jax.sharding import Mesh, PartitionSpec as P

outer_rate = 0.7
decay_rate = 0.9

ZH, ZL = 4, 8
NEAR = ("yh", "zl", "core")
REP = ("yh", "zh", "zl", "core")


def powers(exponents):
    return jnp.exp2(exponents.astype(jnp.float32)).astype(jnp.bfloat16).astype(jnp.float32)


def shards(activations, key_cotangent, deltas, delta_scales, global_copy, momentum, code_scales):
    yh, zh, zl, core = [lax.axis_index(name) for name in REP]
    rows, columns = global_copy.shape
    sub = rows // (4 * ZH * ZL)

    decoded = deltas[0].astype(jnp.float32) * powers(delta_scales[0])
    decoded = decoded.astype(jnp.bfloat16).reshape(2, ZH, ZL, 2, sub, columns)
    outgoing = decoded.transpose(0, 2, 3, 1, 4, 5).reshape(rows, columns)
    incoming = lax.all_to_all(outgoing, NEAR, 0, 0, tiled=True)
    near_sum = jnp.sum(incoming.reshape(4 * ZL, ZH * sub, columns).astype(jnp.float32), axis=0)
    summed = lax.psum(near_sum, "zh").reshape(ZH, sub, columns)

    def own(array):
        split = array.reshape(2, ZH, ZL, 2, sub, array.shape[-1])
        part = lax.dynamic_slice(split, (yh, 0, zl, core, 0, 0), (1, ZH, 1, 1, sub, array.shape[-1]))
        return part.reshape(ZH, sub, array.shape[-1])

    outer_grad = -summed / lax.axis_size(REP)
    new_momentum = decay_rate * own(momentum) + outer_grad
    new_global = own(global_copy) - outer_rate * (outer_grad + decay_rate * new_momentum)
    coded = (new_global * powers(-own(code_scales))).astype(jnp.bfloat16)
    spread = jnp.broadcast_to(coded[None], (4 * ZL, ZH, sub, columns)).reshape(rows, columns)
    encoded = lax.all_to_all(spread, NEAR, 0, 0, tiled=True)
    encoded = encoded.reshape(2, ZL, 2, ZH, sub, columns).transpose(0, 3, 1, 2, 4, 5).reshape(rows, columns)

    key_grad = lax.dot_general(
        activations, key_cotangent, (((0,), (0,)), ((), ())), preferred_element_type=jnp.float32
    )
    key_grad = key_grad.astype(jnp.bfloat16)[None]
    pick = lambda array: lax.dynamic_index_in_dim(array, zh, 0, keepdims=False)
    return (key_grad, pick(new_momentum), pick(new_global), encoded)


def solution(mesh):
    devices = mesh.devices
    grid = Mesh(devices.reshape(2, ZH, ZL, 2, devices.shape[1]), (*REP, "fsdp"))
    in_specs = (
        P(REP, None),
        P(REP, "fsdp"),
        P(REP, None, "fsdp"),
        P(REP, None, "fsdp"),
        P(None, "fsdp"),
        P(None, "fsdp"),
        P(None, "fsdp"),
    )
    out_specs = (P(REP, None, "fsdp"), P(REP, "fsdp"), P(REP, "fsdp"), P(None, "fsdp"))
    return jax.shard_map(shards, mesh=grid, in_specs=in_specs, out_specs=out_specs, check_vma=False)
```

time: 1070 us -> 86.4 us (0.08)
  waiting for transfers between devices: 902 us -> 19.5 us
  blocking collectives: 142 us -> 26.2 us
  starting transfers between devices: 0.04 us -> 24.8 us
  between operations: 14.7 us -> 0.74 us
    unnamed x2 -> x0, waiting for transfers between devices: 902 us -> none
    all_gather x1 -> x0, blocking collectives: 142 us -> none  [shards(): encoded = lax.all_gather(coded_share, 'rep', axis=0, tiled=True)]
    psum x0 -> x1, blocking collectives: none -> 26.2 us  [shards(): summed = lax.psum(near_sum, 'zh').reshape(ZH, sub, columns)]
    all_to_all x0 -> x2, starting transfers between devices: none -> 24.8 us  [the longest x1 17.7 us: shards(): incoming = lax.all_to_all(outgoing, NEAR, 0, 0, tiled=True)]
    all_to_all x0 -> x2, waiting for transfers between devices: none -> 19.5 us  [the longest x1 12.6 us: shards(): incoming = lax.all_to_all(outgoing, NEAR, 0, 0, tiled=True)]
  transfers between devices with their start and end apart: 1 -> 2, of which waited for: 1 -> 2; matrix products, arithmetic and copies ran while one was open for 1% -> 11% of each run, Pallas kernels for 0% -> 0%
where the time goes in v1:
time: 86.4 us; the launch traced here: 86 us
  blocking collectives  26.2 us (30%)
  starting transfers between devices  24.8 us (29%)
  waiting for transfers between devices  19.5 us (23%)
  matrix products  7.11 us (8%)
  other arithmetic  5.28 us (6%)
  local copies, waits for them, and re-layouts  2.34 us (3%)
    psum x1, blocking collectives, shards(): summed = lax.psum(near_sum, 'zh').reshape(ZH, sub, columns)  26.2 us
    all_to_all x1, starting transfers between devices, shards(): incoming = lax.all_to_all(outgoing, NEAR, 0, 0, tiled=True)  17.7 us
    all_to_all x1, waiting for transfers between devices, shards(): incoming = lax.all_to_all(outgoing, NEAR, 0, 0, tiled=True)  12.6 us
    dot_general x1, matrix products, shards(): lax.dot_general(activations, key_cotangent, (((0,), (0,)), ((), ())), pre...  7.11 us
    all_to_all x1, starting transfers between devices, shards(): encoded = lax.all_to_all(spread, NEAR, 0, 0, tiled=True)  7.09 us
    all_to_all x1, waiting for transfers between devices, shards(): encoded = lax.all_to_all(spread, NEAR, 0, 0, tiled=True)  6.91 us
    convert_element_type x1, other arithmetic, shards(): decoded = decoded.astype(jnp.bfloat16).reshape(2, ZH, ZL, 2, sub, columns)  1.77 us
  transfers between devices with their start and end apart: 2, of which 2 were waited for; matrix products, arithmetic and copies ran while one was open for 11% of the time, Pallas kernels for 0%

profile of v1, /device:TPU:1, one launch (start us, length us, event | category | flops | bytes accessed | tf_op | source)
XLA Modules:
  0.0 86.0 jit_solution(577154605830662727)
XLA Ops:
  0.6 0.0 copy-start
  0.6 0.7 convert_reduce_fusion.1
  1.4 0.1 reshape.136
  1.6 1.8 %fusion.1 = bf16[2,4,8,2,4,128]{5,4,1,3,2,0:T(4,128)(2,1)} fusion(f32[2,4,8,2,4]{4,1,3,2,0:T(4,128)S(1)} %copy.21, bf16[2,4,8,2,4,128]{5,4,3,2,1,0:T(4,128)(2,1)} %bitcast.38), kind=kLoop, calls=%fused_computation.3 | loop fusion | flops 196608 | bytes 264192 | tf_op jit(solution)/shard_map/convert_element_type | solution.py:25
  3.4 17.7 %all-to-all-start = ((bf16[32,16,128]{2,1,0:T(8,128)(2,1)}), bf16[32,16,128]{2,1,0:T(8,128)(2,1)S(1)}, u32[]{:S(2)}, u32[]{:S(2)}) async-start(bf16[32,16,128]{2,1,0:T(8,128)(2,1)} %bitcast.5), calls=%async_computation | async-start | bytes 262144 | tf_op jit(solution)/shard_map/all_to_all | solution.py:27
  21.0 0.5 broadcast.75
  21.6 1.3 %reduce.7 = s32[512]{0:T(512)S(1)} reduce(s32[512,1]{0,1:T(1,128)} %param.13, s32[]{:T(128)} %broadcast.75), dimensions={1}, to_apply=%param.13.reduce_sub_computation.3 | reduce | bytes 4100 | tf_op args[6]
  22.9 0.1 reshape.132
  23.1 0.1 reshape.137
  23.2 0.0 copy-done
  23.2 12.6 %all-to-all-done = bf16[32,16,128]{2,1,0:T(8,128)(2,1)S(1)} async-done(((bf16[32,16,128]{2,1,0:T(8,128)(2,1)}), bf16[32,16,128]{2,1,0:T(8,128)(2,1)S(1)}, u32[]{:S(2)}, u32[]{:S(2)}) %all-to-all-start) | async-done | bytes 131104 | tf_op jit(solution)/shard_map/all_to_all | solution.py:27
  35.8 26.2 %psum.7 = f32[16,128]{1,0:T(8,128)S(1)} all-reduce(f32[16,128]{1,0:T(8,128)S(1)} %convert_reduce_fusion), channel_id=1, replica_groups=mesh['yh'=2,'zh'=4,'zl'=8,'core'=2,'fsdp'=8] {'zh'}, use_global_device_ids=true, to_apply=%region_1.0 | all-reduce | flops 2048 | bytes 16384 | tf_op jit(solution)/shard_map/psum | solution.py:29
  62.1 0.7 bitcast_add_fusion
  62.8 0.1 multiply_convert_fusion
  62.9 0.7 broadcast_in_dim.10
  63.5 7.1 %all-to-all-start.1 = ((bf16[32,16,128]{2,1,0:T(8,128)(2,1)}), bf16[32,16,128]{2,1,0:T(8,128)(2,1)S(1)}, u32[]{:S(2)}, u32[]{:S(2)}) async-start(bf16[32,16,128]{2,1,0:T(8,128)(2,1)} %broadcast_in_dim.10), calls=%async_computation.1 | async-start | bytes 262144 | tf_op jit(solution)/shard_map/all_to_all | solution.py:41
  70.7 7.1 %fusion = bf16[1,8192,128]{2,1,0:T(8,128)(2,1)} fusion(bf16[512,8192]{1,0:T(8,128)(2,1)} %param.7, bf16[512,128]{1,0:T(8,128)(2,1)} %param.8), kind=kOutput, calls=%fused_computation.1 | convolution fusion | flops 1074790400 | bytes 10616832 | tf_op jit(solution)/shard_map/dot_general | solution.py:44
  77.8 0.6 fusion.2
  78.4 6.9 %all-to-all-done.1 = bf16[32,16,128]{2,1,0:T(8,128)(2,1)S(1)} async-done(((bf16[32,16,128]{2,1,0:T(8,128)(2,1)}), bf16[32,16,128]{2,1,0:T(8,128)(2,1)S(1)}, u32[]{:S(2)}, u32[]{:S(2)}) %all-to-all-start.1) | async-done | bytes 131104 | tf_op jit(solution)/shard_map/all_to_all | solution.py:41
  85.3 0.7 copy.24
  (7 shorter events, 0.1 us)
Async XLA Ops:
  0.6 22.5 %copy-start = (f32[512,128]{1,0:T(8,128)S(1)}, f32[512,128]{1,0:T(8,128)}, u32[]{:S(2)}) copy-start(f32[512,128]{1,0:T(8,128)} %param.11) | copy-start | bytes 786436
  3.4 32.4 %all-to-all-start = ((bf16[32,16,128]{2,1,0:T(8,128)(2,1)}), bf16[32,16,128]{2,1,0:T(8,128)(2,1)S(1)}, u32[]{:S(2)}, u32[]{:S(2)}) async-start(bf16[32,16,128]{2,1,0:T(8,128)(2,1)} %bitcast.5), calls=%async_computation | async-start | bytes 262144 | tf_op jit(solution)/shard_map/all_to_all | solution.py:27
  63.5 21.7 %all-to-all-start.1 = ((bf16[32,16,128]{2,1,0:T(8,128)(2,1)}), bf16[32,16,128]{2,1,0:T(8,128)(2,1)S(1)}, u32[]{:S(2)}, u32[]{:S(2)}) async-start(bf16[32,16,128]{2,1,0:T(8,128)(2,1)} %broadcast_in_dim.10), calls=%async_computation.1 | async-start | bytes 262144 | tf_op jit(solution)/shard_map/all_to_all | solution.py:41

commit v2 on v0

v2 whole, which is shorter than its diff:
```python
import jax
import jax.numpy as jnp
from jax import lax
from jax.experimental import pallas as pl
from jax.experimental.pallas import tpu as pltpu
from jax.sharding import PartitionSpec as P

outer_rate = 0.7
decay_rate = 0.9

QUADS, LANES = 4, 8
RING = QUADS * LANES


def member(y_hi, z, core):
    return (y_hi * RING + z % RING) * 2 + core


STEPS = (0, -4, -3, -2, 3, -1, 2, 1)
BACK_STEPS = (0, 1, 2, 3, 4, -3, -2, -1)


def near(steps):
    return [
        [member(y, LANES * quad + step, core) for step in steps for y in (0, 1) for core in (0, 1)]
        for quad in range(QUADS)
    ]


NEAR, BACK = near(STEPS), near(BACK_STEPS)
FAR = [
    [member(y, first + LANES * quad, core) for quad in range(QUADS)]
    for first in (16, 17, 18, 19, 12, 13, 14, 15) for y in (0, 1) for core in (0, 1)
]


def powers(exponents):
    return jnp.exp2(exponents.astype(jnp.float32)).astype(jnp.bfloat16).astype(jnp.float32)


def decode(codes_ref, exponents_ref, out_ref):
    scales = powers(exponents_ref[...])
    block = scales.shape[1]
    rows = []
    for first in range(scales.shape[0]):
        turned = jnp.broadcast_to(scales[first : first + 1], (block, block)).T
        codes = codes_ref[pl.ds(first * block, block), :].astype(jnp.float32)
        rows.append((codes * turned).reshape(block // 8, 8, block))
    tiles = [part[i] for part in rows for i in range(block // 8)]
    low = lax.broadcasted_iota(jnp.int32, tiles[0].shape, 0) < 4
    for place, step in enumerate(STEPS):
        lane = step % LANES
        for y_hi in range(2):
            a, b, c, d = [tiles[(y_hi * QUADS + quad) * LANES + lane] for quad in range(QUADS)]
            first = (place * 2 + y_hi) * 2 * 16
            for core, (even, odd) in enumerate((((a, c), (b, d)), ((a, c), (b, d)))):
                halves = []
                for one, two in zip(even, odd):
                    if core == 0:
                        halves.append(jnp.where(low, one, pltpu.roll(two, 4, 0)))
                    else:
                        halves.append(jnp.where(low, pltpu.roll(one, 4, 0), two))
                out_ref[pl.ds(first + core * 16, 16), :] = jnp.concatenate(halves, axis=0).astype(jnp.bfloat16)


def shards(activations, key_cotangent, deltas, delta_scales, global_copy, momentum, code_scales):
    rep = lax.axis_index("rep")
    y_hi, z, core = rep // (2 * RING), (rep // 2) % RING, rep % 2
    quad, lane = z // LANES, z % LANES
    rows, columns = global_copy.shape
    sub = rows // (4 * RING)
    held = QUADS * sub

    def own(array):
        split = array.reshape(2, QUADS, LANES, 2, sub, array.shape[-1])
        part = lax.dynamic_slice(split, (y_hi, 0, lane, core, 0, 0), (1, QUADS, 1, 1, sub, array.shape[-1]))
        return part.reshape(QUADS, sub, array.shape[-1])

    scales = jnp.broadcast_to(powers(-own(code_scales)), (QUADS, sub, columns)).reshape(held, columns)
    outgoing = pl.pallas_call(
        decode,
        out_shape=jax.ShapeDtypeStruct((rows, columns), jnp.bfloat16),
        in_specs=[pl.BlockSpec(memory_space=pltpu.VMEM)] * 2,
        out_specs=pl.BlockSpec(memory_space=pltpu.VMEM),
        cost_estimate=pl.CostEstimate(flops=rows * columns, bytes_accessed=4 * rows * columns, transcendentals=rows),
    )(deltas[0], delta_scales.reshape(rows // columns, columns))
    outgoing, key_cotangent = lax.optimization_barrier((outgoing, key_cotangent))
    incoming = lax.all_to_all(outgoing, "rep", 0, 0, tiled=True, axis_index_groups=NEAR)
    key_grad = lax.dot_general(
        activations, key_cotangent, (((0,), (0,)), ((), ())), preferred_element_type=jnp.float32
    )
    key_grad = key_grad.astype(jnp.bfloat16)[None]
    incoming, key_grad, moment, base, scales = lax.optimization_barrier(
        (incoming, key_grad, own(momentum), own(global_copy), scales)
    )
    near_sum = jnp.sum(incoming.reshape(4 * LANES, held, columns).astype(jnp.float32), axis=0)
    sums = lax.psum(near_sum, "rep", axis_index_groups=FAR)
    def step(total, moment, base):
        outer_grad = -total / lax.axis_size("rep")
        new_momentum = decay_rate * moment + outer_grad
        return new_momentum, base - outer_rate * (outer_grad + decay_rate * new_momentum)

    moment, base = moment.reshape(held, columns), base.reshape(held, columns)
    copies = lambda array: jnp.broadcast_to(array[None], (4 * LANES, held, columns))
    spread = step(copies(sums), copies(moment), copies(base))[1] * copies(scales)
    spread = spread.astype(jnp.bfloat16).reshape(rows, columns)
    encoded = lax.all_to_all(spread, "rep", 0, 0, tiled=True, axis_index_groups=BACK)
    encoded = encoded.reshape(LANES, 2, 2, QUADS, sub, columns).transpose(1, 3, 0, 2, 4, 5).reshape(rows, columns)

    new_momentum, new_global = step(*[lax.dynamic_slice_in_dim(a, quad * sub, sub, 0) for a in (sums, moment, base)])
    return (key_grad, new_momentum, new_global, encoded)


def solution(mesh):
    in_specs = (
        P("rep", None),
        P("rep", "fsdp"),
        P("rep", None, "fsdp"),
        P("rep", None, "fsdp"),
        P(None, "fsdp"),
        P(None, "fsdp"),
        P(None, "fsdp"),
    )
    out_specs = (P("rep", None, "fsdp"), P("rep", "fsdp"), P("rep", "fsdp"), P(None, "fsdp"))
    return jax.shard_map(shards, mesh=mesh, in_specs=in_specs, out_specs=out_specs, check_vma=False)
```

time: 1070 us -> 79.1 us (0.07)
  waiting for transfers between devices: 902 us -> 12.4 us
  blocking collectives: 142 us -> 19.9 us
  starting transfers between devices: 0.04 us -> 31.8 us
  between operations: 14.7 us -> 0.83 us
    unnamed x2 -> x0, waiting for transfers between devices: 902 us -> none
    all_gather x1 -> x0, blocking collectives: 142 us -> none  [shards(): encoded = lax.all_gather(coded_share, 'rep', axis=0, tiled=True)]
    all_to_all x0 -> x2, starting transfers between devices: none -> 31.8 us  [the longest x1 23.7 us: shards(): lax.all_to_all(outgoing, 'rep', 0, 0, tiled=True, axis_index_groups=NEAR)]
    psum x0 -> x1, blocking collectives: none -> 19.9 us  [shards(): sums = lax.psum(near_sum, 'rep', axis_index_groups=FAR)]
    all_to_all x0 -> x2, waiting for transfers between devices: none -> 12.4 us  [the longest x1 8.3 us: shards(): lax.all_to_all(spread, 'rep', 0, 0, tiled=True, axis_index_groups=BACK)]
  transfers between devices with their start and end apart: 1 -> 2, of which waited for: 1 -> 2; matrix products, arithmetic and copies ran while one was open for 1% -> 13% of each run, Pallas kernels for 0% -> 0%
where the time goes in v2:
time: 79.1 us; the launch traced here: 78.7 us
  starting transfers between devices  31.8 us (40%)
  blocking collectives  19.9 us (25%)
  waiting for transfers between devices  12.4 us (16%)
  local copies, waits for them, and re-layouts  5.37 us (7%)
  matrix products  4.68 us (6%)
  other arithmetic  1.99 us (3%)
  Pallas kernels  1.74 us (2%)
  between operations  0.83 us (1%)
    all_to_all x1, starting transfers between devices, shards(): lax.all_to_all(outgoing, 'rep', 0, 0, tiled=True, axis_index_groups=NEAR)  23.7 us
    psum x1, blocking collectives, shards(): sums = lax.psum(near_sum, 'rep', axis_index_groups=FAR)  19.9 us
    all_to_all x1, waiting for transfers between devices, shards(): lax.all_to_all(spread, 'rep', 0, 0, tiled=True, axis_index_groups=BACK)  8.3 us
    all_to_all x1, starting transfers between devices, shards(): lax.all_to_all(spread, 'rep', 0, 0, tiled=True, axis_index_groups=BACK)  8.16 us
    dot_general x1, matrix products, shards(): lax.dot_general(activations, key_cotangent, (((0,), (0,)), ((), ())), pre...  4.68 us
    all_to_all x1, waiting for transfers between devices, shards(): lax.all_to_all(outgoing, 'rep', 0, 0, tiled=True, axis_index_groups=NEAR)  4.12 us
    unnamed x4, local copies, waits for them, and re-layouts  2.96 us
    pallas_call x1, Pallas kernels, shards(): pl.pallas_call(decode, out_shape=jax.ShapeDtypeStruct((rows, columns), jn...  1.74 us
  transfers between devices with their start and end apart: 2, of which 2 were waited for; matrix products, arithmetic and copies ran while one was open for 13% of the time, Pallas kernels for 0%

profile of v2, /device:TPU:1, one launch (start us, length us, event | category | flops | bytes accessed | tf_op | source)
XLA Modules:
  0.0 78.7 jit_solution(13759520245074313874)
XLA Ops:
  0.6 0.0 copy-start
  0.6 1.7 %shard_map.102 = bf16[512,128]{1,0:T(8,128)(2,1)} custom-call(bf16[512,128]{1,0:T(8,128)(2,1)} %bitcast.30, s32[4,128]{1,0:T(4,128)} %bitcast.37), custom_call_target="tpu_custom_call" | custom-call | flops 65536 | bytes 262144 | tf_op jit(solution)/shard_map/pallas_call | solution.py:80
  2.4 23.7 %all-to-all-start = ((bf16[32,16,128]{2,1,0:T(8,128)(2,1)}), bf16[32,16,128]{2,1,0:T(8,128)(2,1)S(1)}, u32[]{:S(2)}, u32[]{:S(2)}) async-start(bf16[32,16,128]{2,1,0:T(8,128)(2,1)} %bitcast.28), calls=%async_computation | async-start | bytes 262144 | tf_op jit(solution)/shard_map/all_to_all | solution.py:88
  26.1 0.5 broadcast.59
  26.6 1.3 %reduce.3 = s32[512]{0:T(512)S(1)} reduce(s32[512,1]{0,1:T(1,128)} %param.13, s32[]{:T(128)} %broadcast.59), dimensions={1}, to_apply=%param.13.reduce_sub_computation.3 | reduce | bytes 4100 | tf_op args[6]
  28.0 0.1 reshape.88
  28.2 0.1 reshape.93
  28.3 0.7 dynamic-slice_bitcast_fusion
  29.0 0.0 copy-done
  29.0 4.7 %fusion = bf16[1,8192,128]{1,2,0:T(8,128)(2,1)S(1)} fusion(bf16[512,128]{1,0:T(8,128)(2,1)S(1)} %copy-done, bf16[512,8192]{1,0:T(8,128)(2,1)} %param.7), kind=kOutput, calls=%fused_computation.1 | convolution fusion | flops 1074790400 | bytes 10616832 | tf_op jit(solution)/shard_map/dot_general | solution.py:89
  33.7 4.1 %all-to-all-done = bf16[32,16,128]{2,1,0:T(8,128)(2,1)S(1)} async-done(((bf16[32,16,128]{2,1,0:T(8,128)(2,1)}), bf16[32,16,128]{2,1,0:T(8,128)(2,1)S(1)}, u32[]{:S(2)}, u32[]{:S(2)}) %all-to-all-start) | async-done | bytes 131104 | tf_op jit(solution)/shard_map/all_to_all | solution.py:88
  37.8 0.1 broadcast_in_dim.7
  37.9 19.9 %psum.7 = f32[16,128]{1,0:T(8,128)S(1)} all-reduce(f32[16,128]{1,0:T(8,128)S(1)} %convert_reduce_fusion), channel_id=1, replica_groups={{256,384,0,128},{264,392,8,136},{768,896,512,640},{776,904,520,648},{27..., use_global_device_ids=true, to_apply=%region_1.2 | all-reduce | flops 2048 | bytes 16384 | tf_op jit(solution)/shard_map/psum | solution.py:97
  57.8 0.7 broadcast_in_dim.8
  58.5 8.2 %all-to-all-start.1 = ((bf16[32,16,128]{2,1,0:T(8,128)(2,1)}), bf16[32,16,128]{2,1,0:T(8,128)(2,1)S(1)}, u32[]{:S(2)}, u32[]{:S(2)}) async-start(bf16[32,16,128]{2,1,0:T(8,128)(2,1)} %broadcast_in_dim.8), calls=%async_computation.1 | async-start | bytes 262144 | tf_op jit(solution)/shard_map/all_to_all | solution.py:107
  66.7 2.4 %copy.18 = bf16[1,8192,128]{2,1,0:T(8,128)(2,1)} copy(bf16[1,8192,128]{1,2,0:T(8,128)(2,1)S(1)} %fusion) | data formatting | bytes 4194304
  69.2 0.6 multiply_subtract_fusion
  69.7 8.3 %all-to-all-done.1 = bf16[32,16,128]{2,1,0:T(8,128)(2,1)S(1)} async-done(((bf16[32,16,128]{2,1,0:T(8,128)(2,1)}), bf16[32,16,128]{2,1,0:T(8,128)(2,1)S(1)}, u32[]{:S(2)}, u32[]{:S(2)}) %all-to-all-start.1) | async-done | bytes 131104 | tf_op jit(solution)/shard_map/all_to_all | solution.py:107
  78.0 0.7 copy.17
  (4 shorter events, 0.1 us)
Async XLA Ops:
  0.6 28.4 %copy-start = (bf16[512,128]{1,0:T(8,128)(2,1)S(1)}, bf16[512,128]{1,0:T(8,128)(2,1)}, u32[]{:S(2)}) copy-start(bf16[512,128]{1,0:T(8,128)(2,1)} %param.8) | copy-start | bytes 393220
  2.4 35.4 %all-to-all-start = ((bf16[32,16,128]{2,1,0:T(8,128)(2,1)}), bf16[32,16,128]{2,1,0:T(8,128)(2,1)S(1)}, u32[]{:S(2)}, u32[]{:S(2)}) async-start(bf16[32,16,128]{2,1,0:T(8,128)(2,1)} %bitcast.28), calls=%async_computation | async-start | bytes 262144 | tf_op jit(solution)/shard_map/all_to_all | solution.py:88
  58.5 19.5 %all-to-all-start.1 = ((bf16[32,16,128]{2,1,0:T(8,128)(2,1)}), bf16[32,16,128]{2,1,0:T(8,128)(2,1)S(1)}, u32[]{:S(2)}, u32[]{:S(2)}) async-start(bf16[32,16,128]{2,1,0:T(8,128)(2,1)} %broadcast_in_dim.8), calls=%async_computation.1 | async-start | bytes 262144 | tf_op jit(solution)/shard_map/all_to_all | solution.py:107

commit v3 on v2

--- a/solution.py
+++ b/solution.py
@@ -16,21 +16,22 @@
     return (y_hi * RING + z % RING) * 2 + core
 
 
+MIDDLE = 4
 STEPS = (0, -4, -3, -2, 3, -1, 2, 1)
-BACK_STEPS = (0, 1, 2, 3, 4, -3, -2, -1)
+BACK_STEPS = (0, 1, 2, 3, -4, -3, -2, -1)
 
 
-def near(steps):
+def near(steps, middle):
     return [
-        [member(y, LANES * quad + step, core) for step in steps for y in (0, 1) for core in (0, 1)]
+        [member(y, LANES * quad + middle + step, core) for step in steps for y in (0, 1) for core in (0, 1)]
         for quad in range(QUADS)
     ]
 
 
-NEAR, BACK = near(STEPS), near(BACK_STEPS)
+NEAR, BACK = near(STEPS, MIDDLE), near(BACK_STEPS, MIDDLE)
 FAR = [
-    [member(y, first + LANES * quad, core) for quad in range(QUADS)]
-    for first in (16, 17, 18, 19, 12, 13, 14, 15) for y in (0, 1) for core in (0, 1)
+    [member(y, 2 * LANES + lane + LANES * quad, core) for quad in range(QUADS)]
+    for lane in range(LANES) for y in (0, 1) for core in (0, 1)
 ]
 
 
@@ -49,7 +50,7 @@
     tiles = [part[i] for part in rows for i in range(block // 8)]
     low = lax.broadcasted_iota(jnp.int32, tiles[0].shape, 0) < 4
     for place, step in enumerate(STEPS):
-        lane = step % LANES
+        lane = (MIDDLE + step) % LANES
         for y_hi in range(2):
             a, b, c, d = [tiles[(y_hi * QUADS + quad) * LANES + lane] for quad in range(QUADS)]
             first = (place * 2 + y_hi) * 2 * 16
@@ -84,17 +85,12 @@
         out_specs=pl.BlockSpec(memory_space=pltpu.VMEM),
         cost_estimate=pl.CostEstimate(flops=rows * columns, bytes_accessed=4 * rows * columns, transcendentals=rows),
     )(deltas[0], delta_scales.reshape(rows // columns, columns))
-    outgoing, key_cotangent = lax.optimization_barrier((outgoing, key_cotangent))
     incoming = lax.all_to_all(outgoing, "rep", 0, 0, tiled=True, axis_index_groups=NEAR)
-    key_grad = lax.dot_general(
-        activations, key_cotangent, (((0,), (0,)), ((), ())), preferred_element_type=jnp.float32
-    )
-    key_grad = key_grad.astype(jnp.bfloat16)[None]
-    incoming, key_grad, moment, base, scales = lax.optimization_barrier(
-        (incoming, key_grad, own(momentum), own(global_copy), scales)
-    )
+    incoming, moment, base, scales = lax.optimization_barrier((incoming, own(momentum), own(global_copy), scales))
     near_sum = jnp.sum(incoming.reshape(4 * LANES, held, columns).astype(jnp.float32), axis=0)
-    sums = lax.psum(near_sum, "rep", axis_index_groups=FAR)
+    spread = jnp.broadcast_to(near_sum[None], (QUADS, held, columns)).reshape(QUADS * held, columns)
+    parts = lax.all_to_all(spread, "rep", 0, 0, tiled=True, axis_index_groups=FAR)
+    sums = jnp.sum(parts.reshape(QUADS, held, columns), axis=0)
     def step(total, moment, base):
         outer_grad = -total / lax.axis_size("rep")
         new_momentum = decay_rate * moment + outer_grad
@@ -105,9 +101,14 @@
     spread = step(copies(sums), copies(moment), copies(base))[1] * copies(scales)
     spread = spread.astype(jnp.bfloat16).reshape(rows, columns)
     encoded = lax.all_to_all(spread, "rep", 0, 0, tiled=True, axis_index_groups=BACK)
-    encoded = encoded.reshape(LANES, 2, 2, QUADS, sub, columns).transpose(1, 3, 0, 2, 4, 5).reshape(rows, columns)
+    encoded = encoded.reshape(LANES, 2, 2, QUADS, sub, columns).transpose(1, 3, 0, 2, 4, 5)
+    encoded = jnp.concatenate([encoded[:, :, MIDDLE:], encoded[:, :, :MIDDLE]], axis=2).reshape(rows, columns)
 
     new_momentum, new_global = step(*[lax.dynamic_slice_in_dim(a, quad * sub, sub, 0) for a in (sums, moment, base)])
+    key_grad = lax.dot_general(
+        activations, key_cotangent, (((0,), (0,)), ((), ())), preferred_element_type=jnp.float32
+    )
+    key_grad = key_grad.astype(jnp.bfloat16)[None]
     return (key_grad, new_momentum, new_global, encoded)
 
 

time: 79.1 us -> 77.6 us (0.981)
  waiting for transfers between devices: 12.4 us -> 7.49 us
  blocking collectives: 19.9 us -> 23.6 us
  matrix products: 4.68 us -> 7.11 us
  local copies, waits for them, and re-layouts: 5.37 us -> 2.99 us
    all_to_all x0 -> x1, blocking collectives: none -> 23.6 us  [shards(): lax.all_to_all(spread, 'rep', 0, 0, tiled=True, axis_index_groups=FAR)]
    psum x1 -> x0, blocking collectives: 19.9 us -> none  [shards(): sums = lax.psum(near_sum, 'rep', axis_index_groups=FAR)]
    all_to_all x1, waiting for transfers between devices: 8.3 us -> 1.51 us  [shards(): lax.all_to_all(spread, 'rep', 0, 0, tiled=True, axis_index_groups=BACK)]
    all_to_all x1, starting transfers between devices: 23.7 us -> 21.2 us  [shards(): lax.all_to_all(outgoing, 'rep', 0, 0, tiled=True, axis_index_groups=NEAR)]
    unnamed x4 -> x3, local copies, waits for them, and re-layouts: 2.96 us -> 0.52 us
    dot_general x1, matrix products: 4.68 us -> 7.11 us  [shards(): lax.dot_general(activations, key_cotangent, (((0,), (0,)), ((), ())), pre...]
    all_to_all x1, starting transfers between devices: 8.16 us -> 10.2 us  [shards(): lax.all_to_all(spread, 'rep', 0, 0, tiled=True, axis_index_groups=BACK)]
    all_to_all x1, waiting for transfers between devices: 4.12 us -> 5.99 us  [shards(): lax.all_to_all(outgoing, 'rep', 0, 0, tiled=True, axis_index_groups=NEAR)]
  transfers between devices with their start and end apart: 2 -> 2, of which waited for: 2 -> 2; matrix products, arithmetic and copies ran while one was open for 13% -> 14% of each run, Pallas kernels for 0% -> 0%
where the time goes in v3:
time: 77.6 us; the launch traced here: 77.2 us
  starting transfers between devices  31.4 us (40%)
  blocking collectives  23.6 us (30%)
  waiting for transfers between devices  7.49 us (10%)
  matrix products  7.11 us (9%)
  local copies, waits for them, and re-layouts  2.99 us (4%)
  other arithmetic  2.09 us (3%)
  Pallas kernels  1.74 us (2%)
  between operations  0.83 us (1%)
    all_to_all x1, blocking collectives, shards(): lax.all_to_all(spread, 'rep', 0, 0, tiled=True, axis_index_groups=FAR)  23.6 us
    all_to_all x1, starting transfers between devices, shards(): lax.all_to_all(outgoing, 'rep', 0, 0, tiled=True, axis_index_groups=NEAR)  21.2 us
    all_to_all x1, starting transfers between devices, shards(): lax.all_to_all(spread, 'rep', 0, 0, tiled=True, axis_index_groups=BACK)  10.2 us
    dot_general x1, matrix products, shards(): lax.dot_general(activations, key_cotangent, (((0,), (0,)), ((), ())), pre...  7.11 us
    all_to_all x1, waiting for transfers between devices, shards(): lax.all_to_all(outgoing, 'rep', 0, 0, tiled=True, axis_index_groups=NEAR)  5.99 us
    pallas_call x1, Pallas kernels, shards(): pl.pallas_call(decode, out_shape=jax.ShapeDtypeStruct((rows, columns), jn...  1.74 us
  transfers between devices with their start and end apart: 2, of which 2 were waited for; matrix products, arithmetic and copies ran while one was open for 14% of the time, Pallas kernels for 0%

profile of v3, /device:TPU:1, one launch (start us, length us, event | category | flops | bytes accessed | tf_op | source)
XLA Modules:
  0.0 77.2 jit_solution(15378955306212018909)
XLA Ops:
  0.6 0.0 copy-start
  0.6 1.7 %shard_map.102 = bf16[512,128]{1,0:T(8,128)(2,1)} custom-call(bf16[512,128]{1,0:T(8,128)(2,1)} %bitcast.28, s32[4,128]{1,0:T(4,128)} %bitcast.35), custom_call_target="tpu_custom_call" | custom-call | flops 65536 | bytes 262144 | tf_op jit(solution)/shard_map/pallas_call | solution.py:81
  2.4 21.2 %all-to-all-start = ((bf16[32,16,128]{2,1,0:T(8,128)(2,1)}), bf16[32,16,128]{2,1,0:T(8,128)(2,1)S(1)}, u32[]{:S(2)}, u32[]{:S(2)}) async-start(bf16[32,16,128]{2,1,0:T(8,128)(2,1)} %bitcast.26), calls=%async_computation | async-start | bytes 262144 | tf_op jit(solution)/shard_map/all_to_all | solution.py:88
  23.6 0.5 broadcast.60
  24.1 1.3 %reduce.4 = s32[512]{0:T(512)S(1)} reduce(s32[512,1]{0,1:T(1,128)} %param.13, s32[]{:T(128)} %broadcast.60), dimensions={1}, to_apply=%param.13.reduce_sub_computation.3 | reduce | bytes 4100 | tf_op args[6]
  25.5 0.1 reshape.95
  25.7 0.1 reshape.100
  25.8 0.7 dynamic-slice_bitcast_fusion
  26.5 6.0 %all-to-all-done = bf16[32,16,128]{2,1,0:T(8,128)(2,1)S(1)} async-done(((bf16[32,16,128]{2,1,0:T(8,128)(2,1)}), bf16[32,16,128]{2,1,0:T(8,128)(2,1)S(1)}, u32[]{:S(2)}, u32[]{:S(2)}) %all-to-all-start) | async-done | bytes 131104 | tf_op jit(solution)/shard_map/all_to_all | solution.py:88
  32.5 0.1 broadcast_in_dim.9
  32.6 23.6 %all_to_all.24 = f32[4,16,128]{2,1,0:T(8,128)S(1)} all-to-all(f32[4,16,128]{2,1,0:T(8,128)S(1)} %broadcast_in_dim.10), channel_id=1, replica_groups={{256,384,0,128},{264,392,8,136},{768,896,512,640},{776,904,520,648},{27..., dimensions={0} | all-to-all | bytes 65536 | tf_op jit(solution)/shard_map/all_to_all | solution.py:92
  56.2 0.7 broadcast_in_dim.11
  56.9 10.2 %all-to-all-start.2 = ((bf16[32,16,128]{2,1,0:T(8,128)(2,1)}), bf16[32,16,128]{2,1,0:T(8,128)(2,1)S(1)}, u32[]{:S(2)}, u32[]{:S(2)}) async-start(bf16[32,16,128]{2,1,0:T(8,128)(2,1)} %broadcast_in_dim.11), calls=%async_computation.2 | async-start | bytes 262144 | tf_op jit(solution)/shard_map/all_to_all | solution.py:103
  67.2 0.0 copy-done
  67.2 7.1 %fusion = bf16[1,8192,128]{2,1,0:T(8,128)(2,1)} fusion(bf16[512,8192]{1,0:T(8,128)(2,1)} %param.7, bf16[512,128]{1,0:T(8,128)(2,1)S(1)} %copy-done), kind=kOutput, calls=%fused_computation.1 | convolution fusion | flops 1074790400 | bytes 10616832 | tf_op jit(solution)/shard_map/dot_general | solution.py:108
  74.3 0.6 multiply_subtract_fusion
  74.9 1.5 %all-to-all-done.2 = bf16[32,16,128]{2,1,0:T(8,128)(2,1)S(1)} async-done(((bf16[32,16,128]{2,1,0:T(8,128)(2,1)}), bf16[32,16,128]{2,1,0:T(8,128)(2,1)S(1)}, u32[]{:S(2)}, u32[]{:S(2)}) %all-to-all-start.2) | async-done | bytes 131104 | tf_op jit(solution)/shard_map/all_to_all | solution.py:103
  76.4 0.1 pad_maximum_fusion
  76.5 0.7 copy.15
  (7 shorter events, 0.1 us)
Async XLA Ops:
  0.6 66.5 %copy-start = (bf16[512,128]{1,0:T(8,128)(2,1)S(1)}, bf16[512,128]{1,0:T(8,128)(2,1)}, u32[]{:S(2)}) copy-start(bf16[512,128]{1,0:T(8,128)(2,1)} %param.8) | copy-start | bytes 393220
  2.4 30.1 %all-to-all-start = ((bf16[32,16,128]{2,1,0:T(8,128)(2,1)}), bf16[32,16,128]{2,1,0:T(8,128)(2,1)S(1)}, u32[]{:S(2)}, u32[]{:S(2)}) async-start(bf16[32,16,128]{2,1,0:T(8,128)(2,1)} %bitcast.26), calls=%async_computation | async-start | bytes 262144 | tf_op jit(solution)/shard_map/all_to_all | solution.py:88
  56.9 19.5 %all-to-all-start.2 = ((bf16[32,16,128]{2,1,0:T(8,128)(2,1)}), bf16[32,16,128]{2,1,0:T(8,128)(2,1)S(1)}, u32[]{:S(2)}, u32[]{:S(2)}) async-start(bf16[32,16,128]{2,1,0:T(8,128)(2,1)} %broadcast_in_dim.11), calls=%async_computation.2 | async-start | bytes 262144 | tf_op jit(solution)/shard_map/all_to_all | solution.py:103
